TPU v7x, 512 devices: a whole 4x4x16 slice. The times are simulated.
512 devices in a mesh: pipe: 16 (over y_lo, x, core), tensor: 32 (over z, y_hi).
Axes of the slice: x: 4, y: 4 (y_hi: 2, y_lo: 2; y = y_hi * 2 + y_lo), z: 16, core: 2. Of those that a mesh axis runs over, the one named last changes fastest.
Arguments:
- w_up: bfloat16 [29696, 14848], P('tensor', 'pipe'), may hold values from -0.046875 to 0.046875
- inputs_a: bfloat16 [512, 14848], P('tensor', 'pipe'), may hold values from -6 to 6
- grad_a: bfloat16 [512, 29696], P(None, 'tensor'), may hold values from -0.29882812 to 0.29882812
- grad_b: bfloat16 [256, 29696], P(None, 'tensor'), may hold values from -6 to 6
Outputs:
- weight_grad: bfloat16 [29696, 14848], P('tensor', 'pipe')
- input_grad: bfloat16 [256, 14848], P('tensor', 'pipe')
All inputs are finite; a program needn't handle non-finite values.
Results may differ from a plain program's by a relative error of at most 0.0049.
Values may be sent and summed in bfloat16 or wider, within the bound.
A program may use at most 64 MiB of HBM per device.

v0:
```python
import jax
import jax.numpy as jnp
from jax import lax
from jax.sharding import PartitionSpec as P


def slope(pre):
    cdf = 0.5 * (1.0 + jax.scipy.special.erf(pre * 0.7071067811865476))
    pdf = jnp.exp(-0.5 * pre * pre) * 0.3989422804014327
    return cdf + pre * pdf


def project_rows(rows, weight):
    return lax.dot_general(
        rows, weight, (((1,), (1,)), ((), ())), preferred_element_type=jnp.float32
    )


def shards(w_up, inputs_a, grad_a, grad_b):
    gathered = lax.all_gather(inputs_a, "tensor", axis=0, tiled=True)
    partial_pre = project_rows(gathered, w_up)
    pre = lax.psum(partial_pre, "pipe")
    delta = (grad_a.astype(jnp.float32) * slope(pre)).astype(jnp.bfloat16)
    weight_total = lax.dot_general(
        delta, gathered, (((0,), (0,)), ((), ())), preferred_element_type=jnp.float32
    )
    weight_grad = weight_total.astype(jnp.bfloat16)
    input_grad = lax.psum_scatter(
        jnp.dot(grad_b, w_up, preferred_element_type=jnp.float32),
        "tensor",
        scatter_dimension=0,
        tiled=True,
    ).astype(jnp.bfloat16)
    return (weight_grad, input_grad)


def solution(mesh):
    return jax.shard_map(
        shards,
        mesh=mesh,
        in_specs=(P("tensor", "pipe"), P("tensor", "pipe"), P(None, "tensor"), P(None, "tensor")),
        out_specs=(P("tensor", "pipe"), P("tensor", "pipe")),
        check_vma=False,
    )
```

profile of v0, /device:TPU:1, one launch (start us, length us, event | category | flops | bytes accessed | tf_op | source)
XLA Modules:
  0.0 682.4 jit_solution(8484775571471482173)
XLA Ops:
  8.0 0.0 copy-start
  8.0 0.0 copy-start.1
  8.0 0.0 reduce-scatter.2.cloned.1.call-start
  8.1 1.5 copy-done
  9.5 2.7 fusion.18
  12.2 0.0 reduce-scatter.2.cloned.1.call-update
  12.3 0.0 all-reduce.2.cloned.1.call-start
  12.3 0.0 copy-done.1
  12.3 76.1 %all_gather.3 = bf16[512,928]{1,0:T(8,128)(2,1)S(1)} all-gather(bf16[16,928]{1,0:T(8,128)(2,1)S(1)} %copy-done.1), channel_id=1, replica_groups=mesh['pipe'=16,'tensor'=32] {'tensor'}, dimensions={0}, use_global_device_ids=true | all-gather | bytes 979968 | tf_op jit(solution)/shard_map/all_gather | solution.py:20
  88.4 2.4 fusion.17
  90.9 0.0 all-reduce.2.cloned.1.call-update
  90.9 578.1 %reduce-scatter.2.cloned.1.call-done = f32[8,928]{1,0:T(8,128)} async-done(((f32[256,928]{1,0:T(8,128)}), f32[8,928]{1,0:T(8,128)}) %reduce-scatter.2.cloned.1.call-update) | async-done | bytes 29712 | tf_op jit(solution)/shard_map/reduce_scatter | solution.py:28
  669.0 1.4 convert_element_type.15
  670.4 0.0 all-reduce.2.cloned.1.call-done
  670.4 4.5 convolution_convert_fusion
Async XLA Ops:
  8.0 1.5 copy-start
  8.0 4.3 copy-start.1
  8.0 661.0 %reduce-scatter.2.cloned.1.call-start = ((), (), s32[]{:S(2)}) async-start(), calls=%async_computation.2 | async-start | bytes 1081344 | tf_op jit(solution)/shard_map/reduce_scatter | solution.py:28
  12.3 658.1 %all-reduce.2.cloned.1.call-start = ((), (), s32[]{:S(2)}) async-start(), calls=%async_computation.1 | async-start | bytes 3801088 | tf_op jit(solution)/shard_map/psum | solution.py:22
Sparse Core Ops, SparseCore 0:
  13.9 655.1 reduce-scatter.1
Sparse Core Ops, SparseCore 1:
  91.0 144.3 all-reduce.1
where the time goes:
time: 693 us; the launch traced here: 682 us
  waiting for transfers between devices  578 us (83%)
  blocking collectives  76.1 us (11%)
  between operations  15.5 us (2%)
  matrix products  9.7 us (1%)
    reduce_scatter x1, waiting for transfers between devices, shards(): lax.psum_scatter(jnp.dot(grad_b, w_up, preferred_element_type=jnp.float32...  578 us
    all_gather x1, blocking collectives, shards(): gathered = lax.all_gather(inputs_a, 'tensor', axis=0, tiled=True)  76.1 us
  transfers between devices with their start and end apart: 2, of which 1 were waited for; matrix products, arithmetic and copies ran while one was open for 1% of the time, Pallas kernels for 0%

commit v1 on v0

v1 whole, which is shorter than its diff:
```python
import functools

import jax
import jax.numpy as jnp
from jax import lax
from jax.experimental import pallas as pl
from jax.experimental.pallas import tpu as pltpu
from jax.sharding import PartitionSpec as P

MESH = pl.DeviceIdType.MESH
F32 = jnp.float32
BF16 = jnp.bfloat16


def slope(pre):
    cdf = 0.5 * (1.0 + lax.erf(pre * 0.7071067811865476))
    pdf = jnp.exp(-0.5 * pre * pre) * 0.3989422804014327
    return cdf + pre * pdf


class Layout:
    def __init__(self, nz, nx, nyl):
        self.nz, self.nx, self.nyl = nz, nx, nyl
        self.reach = nz // 4
        self.chips = nx * nyl

    def slot(self, dz, yr):
        h, nz = self.reach, self.nz
        dz = (dz + h) % nz - h
        first = dz <= (h if yr == 0 else h - 1) and dz >= (-h if yr == 0 else 1 - h)
        if first:
            return dz + h if yr == 0 else dz + 3 * h
        dz = dz % nz
        return nz + (dz - h - 1 if yr == 0 else dz + h - 1)

    def block_of(self, half, j):
        h, nz = self.reach, self.nz
        if half == 0:
            yr = j // (2 * h + 1)
            return j - h - yr * 2 * h, yr
        yr = (j + nz - (2 * h - 1)) // nz
        return j + h + 1 - 2 * h * yr, yr


def kernel(lay, rows, w_hbm, a_hbm, ga_hbm, gb_hbm, wg_hbm, ig_ref,
           w, g, ga, gb, q, ysend, yrecv, tot, zsend, zrecv,
           p, csend, crecv, own, rsend, rrecv, d, acc, out,
           load_sem, ag_send, ag_recv, y_send, y_recv, z_send, z_recv,
           c_send, c_recv, r_send, r_recv, d_send, d_recv, f_send, f_recv, out_sem):
    nz, nx, nyl = lay.nz, lay.nx, lay.nyl
    tensor, pipe = lax.axis_index("tensor"), lax.axis_index("pipe")
    z, yh = tensor // 2, tensor % 2
    core, chip = pipe % 2, pipe // 2
    yl, x = chip // nx, chip % nx
    half_rows = nz * rows
    core_rows = half_rows // 2

    def at_tensor(dz, dy):
        return {"tensor": ((z + dz + nz) % nz) * 2 + (yh + dy) % 2}

    def at_chip(dyl, dx):
        return {"pipe": (((yl + dyl) % nyl) * nx + (x + dx) % nx) * 2 + core}

    other_core = {"pipe": chip * 2 + (1 - core)}
    others = [(a, b) for a in range(nyl) for b in range(nx) if a or b]

    def remote(src, dst, send, recv, to):
        return pltpu.make_async_remote_copy(
            src_ref=src, dst_ref=dst, send_sem=send, recv_sem=recv, device_id=to, device_id_type=MESH)

    sent = []

    def block(ref, slot):
        return ref.at[pl.ds(slot * rows, rows)]

    load_a = pltpu.make_async_copy(a_hbm, block(g, lay.slot(0, 0)), load_sem.at[0])
    load_w = pltpu.make_async_copy(w_hbm, w, load_sem.at[1])
    load_gb = pltpu.make_async_copy(gb_hbm, gb, load_sem.at[2])
    load_a.start()
    load_w.start()
    load_gb.start()
    load_ga = []
    for half in range(2):
        dz, yr = lay.block_of(half, core * lay.chips + chip)
        t = ((z + dz + nz) % nz) * 2 + (yh + yr) % 2
        c = pltpu.make_async_copy(ga_hbm.at[pl.ds(pl.multiple_of(t * rows, rows), rows)], ga.at[half], load_sem.at[3 + half])
        c.start()
        load_ga.append(c)

    barrier = pltpu.get_barrier_semaphore()
    greet = [at_tensor(dz, 0) for dz in range(1, nz)] + [at_tensor(0, 1), other_core]
    greet += [at_chip(*o) for o in others]
    for to in greet:
        pl.semaphore_signal(barrier, inc=1, device_id=to, device_id_type=MESH)
    pl.semaphore_wait(barrier, len(greet))

    def gather_copy(src, dz, yr, to_left):
        s = lay.slot(dz, yr)
        return remote(src, block(g, s), ag_send.at[s], ag_recv.at[s], at_tensor(-1 if to_left else 1, 0))

    def forward(dz, yr):
        src = block(g, lay.slot(dz, yr))
        last = nz // 2
        for to_left in (True, False):
            if to_left and not (dz >= 0):
                continue
            if not to_left and not (dz <= 0):
                continue
            step = abs(dz) + 1
            if step > last or (step == last and (yr == 0) != to_left):
                continue
            c = gather_copy(a_hbm if (dz == 0 and yr == 0) else src, step if to_left else -step, yr, to_left)
            c.start()
            sent.append(c)

    def arrive(dz, yr):
        s = lay.slot(dz, yr)
        remote(block(g, s), block(g, s), ag_send.at[s], ag_recv.at[s], at_tensor(1, 0)).wait_recv()
        forward(dz, yr)

    s01 = lay.slot(0, 1)
    forward(0, 0)
    c = remote(a_hbm, block(g, s01), ag_send.at[s01], ag_recv.at[s01], at_tensor(0, 1))
    c.start()
    sent.append(c)

    load_gb.wait()
    load_w.wait()
    width = w.shape[1]
    q[...] = jnp.dot(gb[...], w[...], preferred_element_type=F32).reshape(q.shape)
    ysend[...] = q[:, pl.ds(1 - yh, 1)].reshape(nz * q.shape[2], width).astype(BF16)
    yc = remote(ysend, yrecv, y_send, y_recv, at_tensor(0, 1))
    yc.start()
    load_a.wait()

    def sum_b():
        yc.wait_recv()
        tot[:, 0:width] = q[:, pl.ds(yh, 1)].reshape(nz * q.shape[2], width) + yrecv[...].astype(F32)
        wide = 2 * zsend.shape[2]
        if wide > width:
            tot[:, width:wide] = jnp.zeros((tot.shape[0], wide - width), F32)
        left = tot[:, 0:wide // 2].reshape(nz, q.shape[2], wide // 2)
        right = tot[:, wide // 2:wide].reshape(nz, q.shape[2], wide // 2)
        zsend[...] = jnp.concatenate([left, right], axis=1).astype(BF16)

    zcs = []

    def send_b():
        for dz in [s * k for k in range(1, nz // 2 + 1) for s in (1, -1)][:nz - 1]:
            c = remote(zsend.at[(z + dz + nz) % nz], zrecv.at[dz % nz], z_send.at[dz % nz], z_recv.at[dz % nz], at_tensor(dz, 0))
            c.start()
            zcs.append(c)

    def finish_b():
        depth = q.shape[2]
        wide = zsend.shape[2]
        mine = tot[pl.ds(pl.multiple_of(z * depth, depth), depth), :]
        total = jnp.concatenate([mine[:, 0:wide], mine[:, wide:2 * wide]], axis=0)
        for c in zcs:
            c.wait_recv()
        for dz in range(1, nz):
            total += zrecv[dz].astype(F32)
        ig_ref[:, 0:wide] = total[0:depth].astype(BF16)
        ig_ref[:, wide:width] = total[depth:2 * depth, 0:width - wide].astype(BF16)

    core_copies, chip_copies, delta_copies, core_forwards = [None, None], [[], []], [[], []], [[], []]

    def project(half):
        p[half] = lax.dot_general(
            g[pl.ds(half * half_rows, half_rows), :], w[...], (((1,), (1,)), ((), ())), preferred_element_type=F32)
        csend[half] = p[half, pl.ds(pl.multiple_of((1 - core) * core_rows, core_rows), core_rows), :].astype(BF16)
        c = remote(csend.at[half], crecv.at[half], c_send.at[half], c_recv.at[half], other_core)
        c.start()
        core_copies[half] = c

    def reduce_send(half):
        core_copies[half].wait_recv()
        own[half] = p[half, pl.ds(pl.multiple_of(core * core_rows, core_rows), core_rows), :] + crecv[half].astype(F32)
        rsend[half] = own[half].astype(BF16)
        for k, (dyl, dx) in enumerate(others):
            to = ((yl + dyl) % nyl) * nx + (x + dx) % nx
            c = remote(rsend.at[half, pl.ds(pl.multiple_of(to * rows, rows), rows)], rrecv.at[half, k],
                       r_send.at[half, k], r_recv.at[half, k], at_chip(dyl, dx))
            c.start()
            chip_copies[half].append(c)

    def d_block(half, which_core, which_chip):
        start = ((half * 2 + which_core) * lay.chips + which_chip) * rows
        return d.at[pl.ds(pl.multiple_of(start, rows), rows)]

    def activate(half):
        for c in chip_copies[half]:
            c.wait_recv()
        pre = own[half, pl.ds(pl.multiple_of(chip * rows, rows), rows), :]
        for k in range(len(others)):
            pre += rrecv[half, k].astype(F32)
        load_ga[half].wait()
        mine = d_block(half, core, chip)
        mine[...] = (ga[half].astype(F32) * slope(pre)).astype(BF16)
        for k, (dyl, dx) in enumerate(others):
            c = remote(mine, mine, d_send.at[half, k], d_recv.at[half, k], at_chip(dyl, dx))
            c.start()
            delta_copies[half].append(c)
        n = len(others)
        c = remote(mine, mine, f_send.at[half, n], f_recv.at[half, n], other_core)
        c.start()
        core_forwards[half].append(c)

    def spread(half):
        for k, (dyl, dx) in enumerate(others):
            source = ((yl - dyl + nyl) % nyl) * nx + (x - dx + nx) % nx
            b = d_block(half, core, source)
            remote(b, b, d_send.at[half, k], d_recv.at[half, k], at_chip(dyl, dx)).wait_recv()
            c = remote(b, b, f_send.at[half, k], f_recv.at[half, k], other_core)
            c.start()
            core_forwards[half].append(c)

    def collect(half):
        for k, (dyl, dx) in enumerate(others):
            source = ((yl - dyl + nyl) % nyl) * nx + (x - dx + nx) % nx
            b = d_block(half, 1 - core, source)
            remote(b, b, f_send.at[half, k], f_recv.at[half, k], other_core).wait_recv()
        n = len(others)
        b = d_block(half, 1 - core, chip)
        remote(b, b, f_send.at[half, n], f_recv.at[half, n], other_core).wait_recv()

    def weight(half, lo, hi):
        return lax.dot_general(
            d[pl.ds(half * half_rows, half_rows), lo:hi], g[pl.ds(half * half_rows, half_rows), :],
            (((0,), (0,)), ((), ())), preferred_element_type=F32)

    last = nz // 2
    h = lay.reach
    arrive_later = []
    arrive(0, 1)
    for s in range(1, h):
        for yr in (0, 1):
            arrive(s, yr)
            arrive(-s, yr)
    arrive(h, 0)
    arrive(-h, 0)
    project(0)
    if h < last:
        arrive(h, 1)
        arrive(-h, 1)
    reduce_send(0)
    rest = [(s * sign, yr) for s in range(h + 1, last) for yr in (0, 1) for sign in (1, -1)]
    cut = (len(rest) * 2) // 3
    for b in rest[:cut]:
        arrive(*b)
    sum_b()
    activate(0)
    for b in rest[cut:]:
        arrive(*b)
    arrive(last, 0)
    arrive(last, 1)
    project(1)
    spread(0)
    send_b()
    reduce_send(1)
    collect(0)
    hid = w.shape[0]
    cuts = list(range(0, hid, 256)) + [hid]
    for lo, hi in zip(cuts[:-1], cuts[1:]):
        acc[lo:hi, :] = weight(0, lo, hi)
    activate(1)
    spread(1)
    finish_b()
    collect(1)
    outs = []
    for i, (lo, hi) in enumerate(zip(cuts[:-1], cuts[1:])):
        out[lo:hi, :] = (acc[lo:hi, :] + weight(1, lo, hi)).astype(BF16)
        c = pltpu.make_async_copy(out.at[pl.ds(lo, hi - lo)], wg_hbm.at[pl.ds(lo, hi - lo)], out_sem.at[i])
        c.start()
        outs.append(c)
    for c in sent + [yc] + zcs + core_copies + chip_copies[0] + chip_copies[1] + delta_copies[0] + delta_copies[1]:
        c.wait_send()
    for c in core_forwards[0] + core_forwards[1]:
        c.wait_send()
    for c in outs:
        c.wait()


def build(mesh, lay):
    def step(w_up, inputs_a, grad_a, grad_b):
        hid, width = w_up.shape
        rows = inputs_a.shape[0]
        nz = lay.nz
        seq_b = grad_b.shape[0]
        depth = seq_b // (2 * nz)
        half_rows = nz * rows
        n = lay.chips - 1
        wide = -(-width // 256) * 128
        dma = pltpu.SemaphoreType.DMA
        flops = 2 * hid * width * (4 * half_rows + seq_b)
        return pl.pallas_call(
            functools.partial(kernel, lay, rows),
            out_shape=(jax.ShapeDtypeStruct((hid, width), BF16), jax.ShapeDtypeStruct((depth, width), BF16)),
            in_specs=[pl.BlockSpec(memory_space=pl.ANY)] * 4,
            out_specs=(pl.BlockSpec(memory_space=pl.ANY), pl.BlockSpec(memory_space=pltpu.VMEM)),
            scratch_shapes=[
                pltpu.VMEM((hid, width), BF16),
                pltpu.VMEM((2 * half_rows, width), BF16),
                pltpu.VMEM((2, rows, hid), BF16),
                pltpu.VMEM((seq_b, hid), BF16),
                pltpu.VMEM((nz, 2, depth, width), F32),
                pltpu.VMEM((nz * depth, width), BF16),
                pltpu.VMEM((nz * depth, width), BF16),
                pltpu.VMEM((nz * depth, 2 * wide), F32),
                pltpu.VMEM((nz, 2 * depth, wide), BF16),
                pltpu.VMEM((nz, 2 * depth, wide), BF16),
                pltpu.VMEM((2, half_rows, hid), F32),
                pltpu.VMEM((2, half_rows // 2, hid), BF16),
                pltpu.VMEM((2, half_rows // 2, hid), BF16),
                pltpu.VMEM((2, half_rows // 2, hid), F32),
                pltpu.VMEM((2, half_rows // 2, hid), BF16),
                pltpu.VMEM((2, n, rows, hid), BF16),
                pltpu.VMEM((2 * half_rows, hid), BF16),
                pltpu.VMEM((hid, width), F32),
                pltpu.VMEM((hid, width), BF16),
                dma((5,)), dma((2 * nz,)), dma((2 * nz,)), dma, dma, dma((nz,)), dma((nz,)),
                dma((2,)), dma((2,)), dma((2, n)), dma((2, n)), dma((2, n)), dma((2, n)), dma((2, n + 1)), dma((2, n + 1)), dma((8,)),
            ],
            compiler_params=pltpu.CompilerParams(
                collective_id=0, has_side_effects=True, vmem_limit_bytes=40 * 1024 * 1024),
            cost_estimate=pl.CostEstimate(flops=flops, bytes_accessed=5_000_000, transcendentals=100_000),
        )(w_up, inputs_a, grad_a, grad_b)

    return jax.shard_map(
        step,
        mesh=mesh,
        in_specs=(P("tensor", "pipe"), P("tensor", "pipe"), P(None, "tensor"), P(None, "tensor")),
        out_specs=(P("tensor", "pipe"), P("tensor", "pipe")),
        check_vma=False,
    )


def solution(mesh):
    nz = mesh.shape["tensor"] // 2
    nyl = 2
    return build(mesh, Layout(nz, mesh.shape["pipe"] // (2 * nyl), nyl))
```

time: 693 us -> 71.9 us (0.10); the launches traced: 682 us -> 71.7 us
  waiting for transfers between devices: 578 us -> 0 us
  blocking collectives: 76.1 us -> 0 us
  Pallas kernels: 0 us -> 66.3 us
  between operations: 15.5 us -> 0.68 us
  matrix products: 9.7 us -> 0 us
    reduce_scatter x1 -> x0, waiting for transfers between devices: 578 us -> none  [shards(): lax.psum_scatter(jnp.dot(grad_b, w_up, preferred_element_type=jnp.float32...]
    all_gather x1 -> x0, blocking collectives: 76.1 us -> none  [shards(): gathered = lax.all_gather(inputs_a, 'tensor', axis=0, tiled=True)]
    pallas_call x0 -> x1, Pallas kernels: none -> 66.3 us  [step(): pl.pallas_call(functools.partial(kernel, lay, rows), out_shape=(jax.Shape...]
    dot_general x3 -> x0, matrix products: 9.7 us -> none  [the longest x1 4.55 us: shards(): lax.dot_general(delta, gathered, (((0,), (0,)), ((), ())), preferred_elem...]
  transfers between devices with their start and end apart: 2 -> 0, of which waited for: 1 -> 0; matrix products, arithmetic and copies ran while one was open for 1% -> 0% of each run, Pallas kernels for 0% -> 0%
where the time goes in v1:
time: 71.9 us; the launch traced here: 71.7 us
  Pallas kernels  66.3 us (92%)
  local copies, waits for them, and re-layouts  4.72 us (7%)
    pallas_call x1, Pallas kernels, step(): pl.pallas_call(functools.partial(kernel, lay, rows), out_shape=(jax.Shape...  66.3 us
    unnamed x8, local copies, waits for them, and re-layouts  4.72 us

profile of v1, /device:TPU:1, one launch (start us, length us, event | category | flops | bytes accessed | tf_op | source)
XLA Modules:
  0.0 71.7 jit_solution(8283978456706206282)
XLA Ops:
  0.6 0.0 copy-start.1
  0.6 0.0 copy-start
  0.6 1.4 %copy.7.gb_hbm = bf16[256,928]{1,0:T(8,128)(2,1)S(1)} copy(bf16[256,928]{0,1:T(8,128)(2,1)} %param.7) | data formatting | bytes 950272 | tf_op args[3]
  2.0 1.5 %copy.6.ga_hbm = bf16[512,928]{1,0:T(8,128)(2,1)S(1)} copy(bf16[512,928]{0,1:T(8,128)(2,1)} %param.6) | data formatting | bytes 1900544 | tf_op args[2]
  3.5 0.0 copy-done.1
  3.5 0.0 copy-done
  3.5 66.3 %shard_map.59 = (bf16[928,928]{1,0:T(8,128)(2,1)S(1)}, bf16[8,928]{1,0:T(8,128)(2,1)S(1)}) custom-call(bf16[928,928]{1,0:T(8,128)(2,1)S(1)} %copy-done, bf16[16,928]{1,0:T(8,128)(2,1)S(1)} %copy-done.1, bf16[512,928]{1,0:T(8,128)(2,1)S(1)} %copy.6.ga_hbm, bf16[256,928]{1,0:T(8,128)(2,1)S(1)} %copy.7.gb_hbm), custom_call_target="tpu_custom_call" | custom-call | flops 2204631040 | bytes 5000000 | tf_op jit(solution)/shard_map/pallas_call | solution.py:296
  69.8 1.3 %copy.10 = bf16[928,928]{1,0:T(8,128)(2,1)} copy(bf16[928,928]{1,0:T(8,128)(2,1)S(1)} %get-tuple-element.4) | data formatting | bytes 3444736
  71.1 0.6 copy.11
Async XLA Ops:
  0.6 2.9 %copy-start.1 = (bf16[16,928]{1,0:T(8,128)(2,1)S(1)}, bf16[16,928]{1,0:T(8,128)(2,1)}, u32[]{:S(2)}) copy-start(bf16[16,928]{1,0:T(8,128)(2,1)} %a_hbm.1) | copy-start | bytes 89092
  0.6 2.9 %copy-start = (bf16[928,928]{1,0:T(8,128)(2,1)S(1)}, bf16[928,928]{1,0:T(8,128)(2,1)}, u32[]{:S(2)}) copy-start(bf16[928,928]{1,0:T(8,128)(2,1)} %w_hbm.1) | copy-start | bytes 5167108

commit v2 on v1

--- a/solution.py
+++ b/solution.py
@@ -21,29 +21,22 @@
 class Layout:
     def __init__(self, nz, nx, nyl):
         self.nz, self.nx, self.nyl = nz, nx, nyl
-        self.reach = nz // 4
         self.chips = nx * nyl
+        last = nz // 2
+        self.direct = (6, 3, 1) if nz == 16 else (1,)
+        self.relays = {1: (2,), 3: (4,), 6: (8, 7, 5)} if nz == 16 else {1: (2,)}
+        distances = (1, 3, 6, 2, 4, 5, 7) if nz == 16 else (1,)
+        arrivals = [0] + [d * s for d in distances for s in (1, -1)] + [nz // 2]
+        order = [(d, yr) for yr in (0, 1) for d in arrivals]
+        self.order = order
 
     def slot(self, dz, yr):
-        h, nz = self.reach, self.nz
-        dz = (dz + h) % nz - h
-        first = dz <= (h if yr == 0 else h - 1) and dz >= (-h if yr == 0 else 1 - h)
-        if first:
-            return dz + h if yr == 0 else dz + 3 * h
-        dz = dz % nz
-        return nz + (dz - h - 1 if yr == 0 else dz + h - 1)
-
-    def block_of(self, half, j):
-        h, nz = self.reach, self.nz
-        if half == 0:
-            yr = j // (2 * h + 1)
-            return j - h - yr * 2 * h, yr
-        yr = (j + nz - (2 * h - 1)) // nz
-        return j + h + 1 - 2 * h * yr, yr
+        dz = dz % self.nz
+        return self.order.index((dz if dz <= self.nz // 2 else dz - self.nz, yr))
 
 
 def kernel(lay, rows, w_hbm, a_hbm, ga_hbm, gb_hbm, wg_hbm, ig_ref,
-           w, g, ga, gb, q, ysend, yrecv, tot, zsend, zrecv,
+           w, g, ga, gat, gb, q, ysend, yrecv, tot, zsend, zrecv,
            p, csend, crecv, own, rsend, rrecv, d, acc, out,
            load_sem, ag_send, ag_recv, y_send, y_recv, z_send, z_recv,
            c_send, c_recv, r_send, r_recv, d_send, d_recv, f_send, f_recv, out_sem):
@@ -70,22 +63,29 @@
 
     sent = []
 
-    def block(ref, slot):
-        return ref.at[pl.ds(slot * rows, rows)]
-
-    load_a = pltpu.make_async_copy(a_hbm, block(g, lay.slot(0, 0)), load_sem.at[0])
+    def block(slot):
+        return g.at[pl.ds(slot * rows, rows)]
+
+    load_a = pltpu.make_async_copy(a_hbm, block(lay.slot(0, 0)), load_sem.at[0])
     load_w = pltpu.make_async_copy(w_hbm, w, load_sem.at[1])
     load_gb = pltpu.make_async_copy(gb_hbm, gb, load_sem.at[2])
     load_a.start()
     load_w.start()
     load_gb.start()
-    load_ga = []
+    load_ga, ga_row = [], []
+    lanes = ga.shape[2]
     for half in range(2):
-        dz, yr = lay.block_of(half, core * lay.chips + chip)
-        t = ((z + dz + nz) % nz) * 2 + (yh + yr) % 2
-        c = pltpu.make_async_copy(ga_hbm.at[pl.ds(pl.multiple_of(t * rows, rows), rows)], ga.at[half], load_sem.at[3 + half])
+        dz, yr = 0, 0
+        for j in range(nz):
+            hit = 1 - jnp.minimum(jnp.abs(core * lay.chips + chip - j), 1)
+            block_z, block_y = lay.order[half * nz + j]
+            dz, yr = dz + hit * (block_z % nz), yr + hit * block_y
+        t = ((z + dz) % nz) * 2 + (yh + yr) % 2
+        start = pl.multiple_of((t * rows // lanes) * lanes, lanes)
+        c = pltpu.make_async_copy(ga_hbm.at[:, pl.ds(start, lanes)], ga.at[half], load_sem.at[3 + half])
         c.start()
         load_ga.append(c)
+        ga_row.append(pl.multiple_of(t * rows % lanes, rows))
 
     barrier = pltpu.get_barrier_semaphore()
     greet = [at_tensor(dz, 0) for dz in range(1, nz)] + [at_tensor(0, 1), other_core]
@@ -94,44 +94,48 @@
         pl.semaphore_signal(barrier, inc=1, device_id=to, device_id_type=MESH)
     pl.semaphore_wait(barrier, len(greet))
 
-    def gather_copy(src, dz, yr, to_left):
+    def gather(src, dz, yr, to):
         s = lay.slot(dz, yr)
-        return remote(src, block(g, s), ag_send.at[s], ag_recv.at[s], at_tensor(-1 if to_left else 1, 0))
-
-    def forward(dz, yr):
-        src = block(g, lay.slot(dz, yr))
-        last = nz // 2
-        for to_left in (True, False):
-            if to_left and not (dz >= 0):
-                continue
-            if not to_left and not (dz <= 0):
-                continue
-            step = abs(dz) + 1
-            if step > last or (step == last and (yr == 0) != to_left):
-                continue
-            c = gather_copy(a_hbm if (dz == 0 and yr == 0) else src, step if to_left else -step, yr, to_left)
-            c.start()
-            sent.append(c)
+        return remote(src, block(s), ag_send.at[s], ag_recv.at[s], to)
+
+    def start_gather():
+        copies = [gather(a_hbm, d * s, 0, at_tensor(-d * s, 0)) for d in lay.direct for s in (1, -1)]
+        copies.insert(2, gather(a_hbm, 0, 1, at_tensor(0, 1)))
+        for c in copies:
+            c.start()
+        sent.extend(copies)
 
     def arrive(dz, yr):
-        s = lay.slot(dz, yr)
-        remote(block(g, s), block(g, s), ag_send.at[s], ag_recv.at[s], at_tensor(1, 0)).wait_recv()
-        forward(dz, yr)
-
-    s01 = lay.slot(0, 1)
-    forward(0, 0)
-    c = remote(a_hbm, block(g, s01), ag_send.at[s01], ag_recv.at[s01], at_tensor(0, 1))
-    c.start()
-    sent.append(c)
-
-    load_gb.wait()
-    load_w.wait()
+        src = block(lay.slot(dz, yr))
+        gather(src, dz, yr, at_tensor(1, 0)).wait_recv()
+        if yr == 0:
+            sign = 1 if dz > 0 else -1
+            copies = []
+            for d in lay.relays.get(abs(dz), ()):
+                if d < nz // 2 or dz > 0:
+                    copies.append(gather(src, d * sign, 0, at_tensor(dz - d * sign, 0)))
+            copies.append(gather(src, dz, 1, at_tensor(0, 1)))
+            for c in copies:
+                c.start()
+            sent.extend(copies)
+
     width = w.shape[1]
-    q[...] = jnp.dot(gb[...], w[...], preferred_element_type=F32).reshape(q.shape)
-    ysend[...] = q[:, pl.ds(1 - yh, 1)].reshape(nz * q.shape[2], width).astype(BF16)
     yc = remote(ysend, yrecv, y_send, y_recv, at_tensor(0, 1))
-    yc.start()
-    load_a.wait()
+
+    def local_b():
+        load_gb.wait()
+        load_w.wait()
+        q[...] = lax.dot_general(gb[...], w[...], (((0,), (0,)), ((), ())), preferred_element_type=F32).reshape(q.shape)
+        ysend[...] = q[:, pl.ds(1 - yh, 1)].reshape(nz * q.shape[2], width).astype(BF16)
+
+    def exchange_b():
+        yc.start()
+        sent.append(yc)
+
+    def turn_ga():
+        for half in range(2):
+            load_ga[half].wait()
+            gat[half] = ga[half].T
 
     def sum_b():
         yc.wait_recv()
@@ -194,9 +198,8 @@
         pre = own[half, pl.ds(pl.multiple_of(chip * rows, rows), rows), :]
         for k in range(len(others)):
             pre += rrecv[half, k].astype(F32)
-        load_ga[half].wait()
         mine = d_block(half, core, chip)
-        mine[...] = (ga[half].astype(F32) * slope(pre)).astype(BF16)
+        mine[...] = (gat[half, pl.ds(ga_row[half], rows), :].astype(F32) * slope(pre)).astype(BF16)
         for k, (dyl, dx) in enumerate(others):
             c = remote(mine, mine, d_send.at[half, k], d_recv.at[half, k], at_chip(dyl, dx))
             c.start()
@@ -229,51 +232,46 @@
             d[pl.ds(half * half_rows, half_rows), lo:hi], g[pl.ds(half * half_rows, half_rows), :],
             (((0,), (0,)), ((), ())), preferred_element_type=F32)
 
-    last = nz // 2
-    h = lay.reach
-    arrive_later = []
-    arrive(0, 1)
-    for s in range(1, h):
-        for yr in (0, 1):
-            arrive(s, yr)
-            arrive(-s, yr)
-    arrive(h, 0)
-    arrive(-h, 0)
+    hid = w.shape[0]
+    cuts = list(range(0, hid, 256)) + [hid]
+    outs = []
+
+    def weigh(half):
+        if half == 0:
+            for lo, hi in zip(cuts[:-1], cuts[1:]):
+                acc[lo:hi, :] = weight(0, lo, hi)
+            return
+        for i, (lo, hi) in enumerate(zip(cuts[:-1], cuts[1:])):
+            out[lo:hi, :] = (acc[lo:hi, :] + weight(1, lo, hi)).astype(BF16)
+            c = pltpu.make_async_copy(out.at[pl.ds(lo, hi - lo)], wg_hbm.at[pl.ds(lo, hi - lo)], out_sem.at[i])
+            c.start()
+            outs.append(c)
+
+    start_gather()
+    local_b()
+    exchange_b()
+    for b in lay.order[1:nz]:
+        arrive(*b)
+    load_a.wait()
     project(0)
-    if h < last:
-        arrive(h, 1)
-        arrive(-h, 1)
+    turn_ga()
     reduce_send(0)
-    rest = [(s * sign, yr) for s in range(h + 1, last) for yr in (0, 1) for sign in (1, -1)]
-    cut = (len(rest) * 2) // 3
-    for b in rest[:cut]:
+    for b in lay.order[nz:]:
         arrive(*b)
+    project(1)
     sum_b()
-    activate(0)
-    for b in rest[cut:]:
-        arrive(*b)
-    arrive(last, 0)
-    arrive(last, 1)
-    project(1)
-    spread(0)
     send_b()
     reduce_send(1)
+    activate(0)
+    activate(1)
+    spread(0)
+    finish_b()
     collect(0)
-    hid = w.shape[0]
-    cuts = list(range(0, hid, 256)) + [hid]
-    for lo, hi in zip(cuts[:-1], cuts[1:]):
-        acc[lo:hi, :] = weight(0, lo, hi)
-    activate(1)
+    weigh(0)
     spread(1)
-    finish_b()
     collect(1)
-    outs = []
-    for i, (lo, hi) in enumerate(zip(cuts[:-1], cuts[1:])):
-        out[lo:hi, :] = (acc[lo:hi, :] + weight(1, lo, hi)).astype(BF16)
-        c = pltpu.make_async_copy(out.at[pl.ds(lo, hi - lo)], wg_hbm.at[pl.ds(lo, hi - lo)], out_sem.at[i])
-        c.start()
-        outs.append(c)
-    for c in sent + [yc] + zcs + core_copies + chip_copies[0] + chip_copies[1] + delta_copies[0] + delta_copies[1]:
+    weigh(1)
+    for c in sent + zcs + core_copies + chip_copies[0] + chip_copies[1] + delta_copies[0] + delta_copies[1]:
         c.wait_send()
     for c in core_forwards[0] + core_forwards[1]:
         c.wait_send()
@@ -301,8 +299,9 @@
             scratch_shapes=[
                 pltpu.VMEM((hid, width), BF16),
                 pltpu.VMEM((2 * half_rows, width), BF16),
-                pltpu.VMEM((2, rows, hid), BF16),
-                pltpu.VMEM((seq_b, hid), BF16),
+                pltpu.VMEM((2, hid, 128), BF16),
+                pltpu.VMEM((2, 128, hid), BF16),
+                pltpu.VMEM((hid, seq_b), BF16),
                 pltpu.VMEM((nz, 2, depth, width), F32),
                 pltpu.VMEM((nz * depth, width), BF16),
                 pltpu.VMEM((nz * depth, width), BF16),
@@ -322,9 +321,9 @@
                 dma((2,)), dma((2,)), dma((2, n)), dma((2, n)), dma((2, n)), dma((2, n)), dma((2, n + 1)), dma((2, n + 1)), dma((8,)),
             ],
             compiler_params=pltpu.CompilerParams(
-                collective_id=0, has_side_effects=True, vmem_limit_bytes=40 * 1024 * 1024),
+                collective_id=0, has_side_effects=True, vmem_limit_bytes=62 * 1024 * 1024),
             cost_estimate=pl.CostEstimate(flops=flops, bytes_accessed=5_000_000, transcendentals=100_000),
-        )(w_up, inputs_a, grad_a, grad_b)
+        )(w_up, inputs_a, grad_a.T, grad_b.T)
 
     return jax.shard_map(
         step,

time: 71.9 us -> 64.7 us (0.90)
  Pallas kernels: 66.3 us -> 60.1 us
  local copies, waits for them, and re-layouts: 4.72 us -> 3.54 us
    pallas_call x1, Pallas kernels: 66.3 us -> 60.1 us  [step(): pl.pallas_call(functools.partial(kernel, lay, rows), out_shape=(jax.Shape...]
    unnamed x8 -> x4, local copies, waits for them, and re-layouts: 4.72 us -> 3.54 us
where the time goes in v2:
time: 64.7 us; the launch traced here: 64.3 us
  Pallas kernels  60.1 us (93%)
  local copies, waits for them, and re-layouts  3.54 us (5%)
  between operations  0.65 us (1%)
    pallas_call x1, Pallas kernels, step(): pl.pallas_call(functools.partial(kernel, lay, rows), out_shape=(jax.Shape...  60.1 us
    unnamed x4, local copies, waits for them, and re-layouts  3.54 us

profile of v2, /device:TPU:1, one launch (start us, length us, event | category | flops | bytes accessed | tf_op | source)
XLA Modules:
  0.0 64.3 jit_solution(14509548282654855018)
XLA Ops:
  0.6 60.1 %shard_map.59 = (bf16[928,928]{1,0:T(8,128)(2,1)}, bf16[8,928]{1,0:T(8,128)(2,1)}) custom-call(bf16[928,928]{1,0:T(8,128)(2,1)} %w_hbm.1, bf16[16,928]{1,0:T(8,128)(2,1)} %a_hbm.1, bf16[928,512]{1,0:T(8,128)(2,1)} %bitcast.2, bf16[928,256]{1,0:T(8,128)(2,1)} %bitcast.3), custom_call_target="tpu_custom_call" | custom-call | flops 2204631040 | bytes 5000000 | tf_op jit(solution)/shard_map/pallas_call | solution.py:294
  60.7 0.0 copy-start
  60.7 2.9 %copy.8 = bf16[928,928]{1,0:T(8,128)(2,1)} copy(bf16[928,928]{1,0:T(8,128)(2,1)} %get-tuple-element.4) | data formatting | bytes 3444736
  63.7 0.0 copy-done
  63.7 0.6 copy.9
Async XLA Ops:
  60.7 2.9 %copy-start = (bf16[8,928]{1,0:T(8,128)(2,1)S(1)}, bf16[8,928]{1,0:T(8,128)(2,1)}, u32[]{:S(2)}) copy-start(bf16[8,928]{1,0:T(8,128)(2,1)} %get-tuple-element.5) | copy-start | bytes 44548

commit v3 on v2

--- a/solution.py
+++ b/solution.py
@@ -23,9 +23,9 @@
         self.nz, self.nx, self.nyl = nz, nx, nyl
         self.chips = nx * nyl
         last = nz // 2
-        self.direct = (6, 3, 1) if nz == 16 else (1,)
-        self.relays = {1: (2,), 3: (4,), 6: (8, 7, 5)} if nz == 16 else {1: (2,)}
-        distances = (1, 3, 6, 2, 4, 5, 7) if nz == 16 else (1,)
+        self.direct = (3, 1) if nz == 16 else (1,)
+        self.relays = {1: (2,), 3: (6, 4), 6: (8, 7, 5)} if nz == 16 else {1: (2,)}
+        distances = (1, 3, 2, 4, 6, 5, 7) if nz == 16 else (1,)
         arrivals = [0] + [d * s for d in distances for s in (1, -1)] + [nz // 2]
         order = [(d, yr) for yr in (0, 1) for d in arrivals]
         self.order = order
@@ -35,11 +35,11 @@
         return self.order.index((dz if dz <= self.nz // 2 else dz - self.nz, yr))
 
 
-def kernel(lay, rows, w_hbm, a_hbm, ga_hbm, gb_hbm, wg_hbm, ig_ref,
+def kernel(lay, rows, w_hbm, a_hbm, ga_hbm, gb_hbm, wg_ref, ig_ref,
            w, g, ga, gat, gb, q, ysend, yrecv, tot, zsend, zrecv,
-           p, csend, crecv, own, rsend, rrecv, d, acc, out,
+           p, csend, crecv, own, rsend, rrecv, d, acc,
            load_sem, ag_send, ag_recv, y_send, y_recv, z_send, z_recv,
-           c_send, c_recv, r_send, r_recv, d_send, d_recv, f_send, f_recv, out_sem):
+           c_send, c_recv, r_send, r_recv, d_send, d_recv, f_send, f_recv):
     nz, nx, nyl = lay.nz, lay.nx, lay.nyl
     tensor, pipe = lax.axis_index("tensor"), lax.axis_index("pipe")
     z, yh = tensor // 2, tensor % 2
@@ -88,7 +88,7 @@
         ga_row.append(pl.multiple_of(t * rows % lanes, rows))
 
     barrier = pltpu.get_barrier_semaphore()
-    greet = [at_tensor(dz, 0) for dz in range(1, nz)] + [at_tensor(0, 1), other_core]
+    greet = [at_tensor(dz, 0) for d in range(1, min(4, nz // 2)) for dz in (d, -d)] + [at_tensor(0, 1), other_core]
     greet += [at_chip(*o) for o in others]
     for to in greet:
         pl.semaphore_signal(barrier, inc=1, device_id=to, device_id_type=MESH)
@@ -100,7 +100,7 @@
 
     def start_gather():
         copies = [gather(a_hbm, d * s, 0, at_tensor(-d * s, 0)) for d in lay.direct for s in (1, -1)]
-        copies.insert(2, gather(a_hbm, 0, 1, at_tensor(0, 1)))
+        copies.insert(len(copies) - 2, gather(a_hbm, 0, 1, at_tensor(0, 1)))
         for c in copies:
             c.start()
         sent.extend(copies)
@@ -234,18 +234,14 @@
 
     hid = w.shape[0]
     cuts = list(range(0, hid, 256)) + [hid]
-    outs = []
 
     def weigh(half):
         if half == 0:
             for lo, hi in zip(cuts[:-1], cuts[1:]):
                 acc[lo:hi, :] = weight(0, lo, hi)
             return
-        for i, (lo, hi) in enumerate(zip(cuts[:-1], cuts[1:])):
-            out[lo:hi, :] = (acc[lo:hi, :] + weight(1, lo, hi)).astype(BF16)
-            c = pltpu.make_async_copy(out.at[pl.ds(lo, hi - lo)], wg_hbm.at[pl.ds(lo, hi - lo)], out_sem.at[i])
-            c.start()
-            outs.append(c)
+        for lo, hi in zip(cuts[:-1], cuts[1:]):
+            wg_ref[lo:hi, :] = (acc[lo:hi, :] + weight(1, lo, hi)).astype(BF16)
 
     start_gather()
     local_b()
@@ -275,8 +271,6 @@
         c.wait_send()
     for c in core_forwards[0] + core_forwards[1]:
         c.wait_send()
-    for c in outs:
-        c.wait()
 
 
 def build(mesh, lay):
@@ -295,7 +289,7 @@
             functools.partial(kernel, lay, rows),
             out_shape=(jax.ShapeDtypeStruct((hid, width), BF16), jax.ShapeDtypeStruct((depth, width), BF16)),
             in_specs=[pl.BlockSpec(memory_space=pl.ANY)] * 4,
-            out_specs=(pl.BlockSpec(memory_space=pl.ANY), pl.BlockSpec(memory_space=pltpu.VMEM)),
+            out_specs=(pl.BlockSpec(memory_space=pltpu.VMEM), pl.BlockSpec(memory_space=pltpu.VMEM)),
             scratch_shapes=[
                 pltpu.VMEM((hid, width), BF16),
                 pltpu.VMEM((2 * half_rows, width), BF16),
@@ -316,14 +310,13 @@
                 pltpu.VMEM((2, n, rows, hid), BF16),
                 pltpu.VMEM((2 * half_rows, hid), BF16),
                 pltpu.VMEM((hid, width), F32),
-                pltpu.VMEM((hid, width), BF16),
                 dma((5,)), dma((2 * nz,)), dma((2 * nz,)), dma, dma, dma((nz,)), dma((nz,)),
-                dma((2,)), dma((2,)), dma((2, n)), dma((2, n)), dma((2, n)), dma((2, n)), dma((2, n + 1)), dma((2, n + 1)), dma((8,)),
+                dma((2,)), dma((2,)), dma((2, n)), dma((2, n)), dma((2, n)), dma((2, n)), dma((2, n + 1)), dma((2, n + 1)),
             ],
             compiler_params=pltpu.CompilerParams(
-                collective_id=0, has_side_effects=True, vmem_limit_bytes=62 * 1024 * 1024),
+                collective_id=0, has_side_effects=True, vmem_limit_bytes=36 * 1024 * 1024),
             cost_estimate=pl.CostEstimate(flops=flops, bytes_accessed=5_000_000, transcendentals=100_000),
-        )(w_up, inputs_a, grad_a.T, grad_b.T)
+        )(*[pltpu.with_memory_space_constraint(v, pltpu.HBM) for v in (w_up, inputs_a, grad_a.T, grad_b.T)])
 
     return jax.shard_map(
         step,

time: 64.7 us -> 59.4 us (0.918)
  Pallas kernels: 60.1 us -> 56.8 us
  local copies, waits for them, and re-layouts: 3.54 us -> 1.86 us
    pallas_call x1, Pallas kernels: 60.1 us -> 56.8 us  [step(): pl.pallas_call(functools.partial(kernel, lay, rows), out_shape=(jax.Shape...]
    unnamed x4 -> x2, local copies, waits for them, and re-layouts: 3.54 us -> 1.86 us
where the time goes in v3:
time: 59.4 us; the launch traced here: 59.3 us
  Pallas kernels  56.8 us (96%)
  local copies, waits for them, and re-layouts  1.86 us (3%)
  between operations  0.64 us (1%)
    pallas_call x1, Pallas kernels, step(): pl.pallas_call(functools.partial(kernel, lay, rows), out_shape=(jax.Shape...  56.8 us
    unnamed x2, local copies, waits for them, and re-layouts  1.86 us

profile of v3, /device:TPU:1, one launch (start us, length us, event | category | flops | bytes accessed | tf_op | source)
XLA Modules:
  0.0 59.3 jit_solution(7829844690323463946)
XLA Ops:
  0.6 56.8 %shard_map.59 = (bf16[928,928]{1,0:T(8,128)(2,1)S(1)}, bf16[8,928]{1,0:T(8,128)(2,1)S(1)}) custom-call(bf16[928,928]{1,0:T(8,128)(2,1)} %w_hbm.1, bf16[16,928]{1,0:T(8,128)(2,1)} %a_hbm.1, bf16[928,512]{1,0:T(8,128)(2,1)} %bitcast.2, bf16[928,256]{1,0:T(8,128)(2,1)} %bitcast.3), custom_call_target="tpu_custom_call" | custom-call | flops 2204631040 | bytes 5000000 | tf_op jit(solution)/shard_map/pallas_call | solution.py:288
  57.4 1.3 %copy.8 = bf16[928,928]{1,0:T(8,128)(2,1)} copy(bf16[928,928]{1,0:T(8,128)(2,1)S(1)} %get-tuple-element.4) | data formatting | bytes 3444736
  58.7 0.6 %copy.9 = bf16[8,928]{1,0:T(8,128)(2,1)} copy(bf16[8,928]{1,0:T(8,128)(2,1)S(1)} %get-tuple-element.5) | data formatting | bytes 29696

commit v4 on v3

--- a/solution.py
+++ b/solution.py
@@ -25,9 +25,18 @@
         last = nz // 2
         self.direct = (3, 1) if nz == 16 else (1,)
         self.relays = {1: (2,), 3: (6, 4), 6: (8, 7, 5)} if nz == 16 else {1: (2,)}
-        distances = (1, 3, 2, 4, 6, 5, 7) if nz == 16 else (1,)
-        arrivals = [0] + [d * s for d in distances for s in (1, -1)] + [nz // 2]
-        order = [(d, yr) for yr in (0, 1) for d in arrivals]
+        self.last_hop = (5, 7, 8) if nz == 16 else ()
+        self.across = (6,) if nz == 16 else ()
+        last = nz // 2
+        pairs = lambda ds: [d * s for d in ds for s in (1, -1)]
+        if nz == 16:
+            own, other = pairs((1, 3, 2, 4, 6)), pairs((1, 3))
+            own_far, other_far = pairs((5, 7)) + [last], pairs((2, 4, 6, 5, 7)) + [last]
+        else:
+            own, other, own_far, other_far = pairs((1,)), [], [last], pairs((1,)) + [last]
+        self.relayed = [(d, 0) for d in own]
+        order = [(d, 0) for d in [0] + own] + [(d, 1) for d in [0] + other]
+        order = order + [(d, 0) for d in own_far] + [(d, 1) for d in other_far]
         self.order = order
 
     def slot(self, dz, yr):
@@ -66,32 +75,18 @@
     def block(slot):
         return g.at[pl.ds(slot * rows, rows)]
 
+    barrier = pltpu.get_barrier_semaphore()
+    greet = [at_tensor(d * s, 0) for d in lay.direct for s in (1, -1)] + [at_tensor(0, 1), other_core]
+    greet += [at_chip(*o) for o in others]
+    for to in greet:
+        pl.semaphore_signal(barrier, inc=1, device_id=to, device_id_type=MESH)
+
     load_a = pltpu.make_async_copy(a_hbm, block(lay.slot(0, 0)), load_sem.at[0])
     load_w = pltpu.make_async_copy(w_hbm, w, load_sem.at[1])
     load_gb = pltpu.make_async_copy(gb_hbm, gb, load_sem.at[2])
     load_a.start()
     load_w.start()
     load_gb.start()
-    load_ga, ga_row = [], []
-    lanes = ga.shape[2]
-    for half in range(2):
-        dz, yr = 0, 0
-        for j in range(nz):
-            hit = 1 - jnp.minimum(jnp.abs(core * lay.chips + chip - j), 1)
-            block_z, block_y = lay.order[half * nz + j]
-            dz, yr = dz + hit * (block_z % nz), yr + hit * block_y
-        t = ((z + dz) % nz) * 2 + (yh + yr) % 2
-        start = pl.multiple_of((t * rows // lanes) * lanes, lanes)
-        c = pltpu.make_async_copy(ga_hbm.at[:, pl.ds(start, lanes)], ga.at[half], load_sem.at[3 + half])
-        c.start()
-        load_ga.append(c)
-        ga_row.append(pl.multiple_of(t * rows % lanes, rows))
-
-    barrier = pltpu.get_barrier_semaphore()
-    greet = [at_tensor(dz, 0) for d in range(1, min(4, nz // 2)) for dz in (d, -d)] + [at_tensor(0, 1), other_core]
-    greet += [at_chip(*o) for o in others]
-    for to in greet:
-        pl.semaphore_signal(barrier, inc=1, device_id=to, device_id_type=MESH)
     pl.semaphore_wait(barrier, len(greet))
 
     def gather(src, dz, yr, to):
@@ -111,10 +106,13 @@
         if yr == 0:
             sign = 1 if dz > 0 else -1
             copies = []
-            for d in lay.relays.get(abs(dz), ()):
+            reached = abs(dz)
+            for d in lay.relays.get(reached, ()):
                 if d < nz // 2 or dz > 0:
-                    copies.append(gather(src, d * sign, 0, at_tensor(dz - d * sign, 0)))
-            copies.append(gather(src, dz, 1, at_tensor(0, 1)))
+                    for dy in (0, 1) if reached in lay.across else (0,):
+                        copies.append(gather(src, d * sign, dy, at_tensor(dz - d * sign, dy)))
+            if reached not in lay.last_hop:
+                copies.append(gather(src, dz, 1, at_tensor(0, 1)))
             for c in copies:
                 c.start()
             sent.extend(copies)
@@ -131,6 +129,23 @@
     def exchange_b():
         yc.start()
         sent.append(yc)
+
+    load_ga, ga_row = [], []
+    lanes = ga.shape[2]
+
+    def start_ga():
+        for half in range(2):
+            dz, yr = 0, 0
+            for j in range(nz):
+                hit = 1 - jnp.minimum(jnp.abs(core * lay.chips + chip - j), 1)
+                block_z, block_y = lay.order[half * nz + j]
+                dz, yr = dz + hit * (block_z % nz), yr + hit * block_y
+            t = ((z + dz) % nz) * 2 + (yh + yr) % 2
+            start = pl.multiple_of((t * rows // lanes) * lanes, lanes)
+            c = pltpu.make_async_copy(ga_hbm.at[:, pl.ds(start, lanes)], ga.at[half], load_sem.at[3 + half])
+            c.start()
+            load_ga.append(c)
+            ga_row.append(pl.multiple_of(t * rows % lanes, rows))
 
     def turn_ga():
         for half in range(2):
@@ -149,8 +164,8 @@
 
     zcs = []
 
-    def send_b():
-        for dz in [s * k for k in range(1, nz // 2 + 1) for s in (1, -1)][:nz - 1]:
+    def send_b(blocks):
+        for dz in [block_z for block_z, block_y in blocks if block_z and block_y == 0]:
             c = remote(zsend.at[(z + dz + nz) % nz], zrecv.at[dz % nz], z_send.at[dz % nz], z_recv.at[dz % nz], at_tensor(dz, 0))
             c.start()
             zcs.append(c)
@@ -246,26 +261,31 @@
     start_gather()
     local_b()
     exchange_b()
+    start_ga()
+    for b in lay.relayed:
+        arrive(*b)
     for b in lay.order[1:nz]:
-        arrive(*b)
+        if b not in lay.relayed:
+            arrive(*b)
     load_a.wait()
     project(0)
     turn_ga()
+    sum_b()
     reduce_send(0)
+    send_b(lay.order[:nz])
     for b in lay.order[nz:]:
         arrive(*b)
+    send_b(lay.order[nz:])
     project(1)
-    sum_b()
-    send_b()
     reduce_send(1)
     activate(0)
     activate(1)
     spread(0)
-    finish_b()
     collect(0)
     weigh(0)
     spread(1)
     collect(1)
+    finish_b()
     weigh(1)
     for c in sent + zcs + core_copies + chip_copies[0] + chip_copies[1] + delta_copies[0] + delta_copies[1]:
         c.wait_send()

time: 59.4 us -> 55.3 us (0.931)
  Pallas kernels: 56.8 us -> 52.6 us
    pallas_call x1, Pallas kernels: 56.8 us -> 52.6 us  [step(): pl.pallas_call(functools.partial(kernel, lay, rows), out_shape=(jax.Shape...]
where the time goes in v4:
time: 55.3 us; the launch traced here: 55.1 us
  Pallas kernels  52.6 us (95%)
  local copies, waits for them, and re-layouts  1.86 us (3%)
  between operations  0.64 us (1%)
    pallas_call x1, Pallas kernels, step(): pl.pallas_call(functools.partial(kernel, lay, rows), out_shape=(jax.Shape...  52.6 us
    unnamed x2, local copies, waits for them, and re-layouts  1.86 us

profile of v4, /device:TPU:1, one launch (start us, length us, event | category | flops | bytes accessed | tf_op | source)
XLA Modules:
  0.0 55.1 jit_solution(8300843342687841002)
XLA Ops:
  0.6 52.6 %shard_map.59 = (bf16[928,928]{1,0:T(8,128)(2,1)S(1)}, bf16[8,928]{1,0:T(8,128)(2,1)S(1)}) custom-call(bf16[928,928]{1,0:T(8,128)(2,1)} %w_hbm.1, bf16[16,928]{1,0:T(8,128)(2,1)} %a_hbm.1, bf16[928,512]{1,0:T(8,128)(2,1)} %bitcast.2, bf16[928,256]{1,0:T(8,128)(2,1)} %bitcast.3), custom_call_target="tpu_custom_call" | custom-call | flops 2204631040 | bytes 5000000 | tf_op jit(solution)/shard_map/pallas_call | solution.py:308
  53.3 1.3 %copy.8 = bf16[928,928]{1,0:T(8,128)(2,1)} copy(bf16[928,928]{1,0:T(8,128)(2,1)S(1)} %get-tuple-element.4) | data formatting | bytes 3444736
  54.5 0.6 %copy.9 = bf16[8,928]{1,0:T(8,128)(2,1)} copy(bf16[8,928]{1,0:T(8,128)(2,1)S(1)} %get-tuple-element.5) | data formatting | bytes 29696

commit v5 on v4

--- a/solution.py
+++ b/solution.py
@@ -24,13 +24,13 @@
         self.chips = nx * nyl
         last = nz // 2
         self.direct = (3, 1) if nz == 16 else (1,)
-        self.relays = {1: (2,), 3: (6, 4), 6: (8, 7, 5)} if nz == 16 else {1: (2,)}
+        self.relays = {1: (2,), 3: (6, 4), 4: (5,), 6: (8, 7)} if nz == 16 else {1: (2,)}
         self.last_hop = (5, 7, 8) if nz == 16 else ()
-        self.across = (6,) if nz == 16 else ()
+        self.across = (4, 6) if nz == 16 else ()
         last = nz // 2
         pairs = lambda ds: [d * s for d in ds for s in (1, -1)]
         if nz == 16:
-            own, other = pairs((1, 3, 2, 4, 6)), pairs((1, 3))
+            own, other = pairs((3, 1, 4, 2, 6)), pairs((1, 3))
             own_far, other_far = pairs((5, 7)) + [last], pairs((2, 4, 6, 5, 7)) + [last]
         else:
             own, other, own_far, other_far = pairs((1,)), [], [last], pairs((1,)) + [last]
@@ -44,9 +44,9 @@
         return self.order.index((dz if dz <= self.nz // 2 else dz - self.nz, yr))
 
 
-def kernel(lay, rows, w_hbm, a_hbm, ga_hbm, gb_hbm, wg_ref, ig_ref,
+def kernel(lay, rows, w_hbm, a_hbm, ga_hbm, gb_hbm, acc, d_out, g_out, ig_ref,
            w, g, ga, gat, gb, q, ysend, yrecv, tot, zsend, zrecv,
-           p, csend, crecv, own, rsend, rrecv, d, acc,
+           p, csend, crecv, own, rsend, rrecv, d,
            load_sem, ag_send, ag_recv, y_send, y_recv, z_send, z_recv,
            c_send, c_recv, r_send, r_recv, d_send, d_recv, f_send, f_recv):
     nz, nx, nyl = lay.nz, lay.nx, lay.nyl
@@ -65,6 +65,7 @@
 
     other_core = {"pipe": chip * 2 + (1 - core)}
     others = [(a, b) for a in range(nyl) for b in range(nx) if a or b]
+    others.sort(key=lambda o: -(o[0] + min(o[1], nx - o[1])))
 
     def remote(src, dst, send, recv, to):
         return pltpu.make_async_remote_copy(
@@ -108,9 +109,10 @@
             copies = []
             reached = abs(dz)
             for d in lay.relays.get(reached, ()):
-                if d < nz // 2 or dz > 0:
-                    for dy in (0, 1) if reached in lay.across else (0,):
-                        copies.append(gather(src, d * sign, dy, at_tensor(dz - d * sign, dy)))
+                for dy in (0, 1) if reached in lay.across else (0,):
+                    if d < nz // 2 or (dz > 0) == (dy == 0) or reached not in lay.across:
+                        if d < nz // 2 or dz > 0 or reached in lay.across:
+                            copies.append(gather(src, d * sign, dy, at_tensor(dz - d * sign, dy)))
             if reached not in lay.last_hop:
                 copies.append(gather(src, dz, 1, at_tensor(0, 1)))
             for c in copies:
@@ -165,7 +167,7 @@
     zcs = []
 
     def send_b(blocks):
-        for dz in [block_z for block_z, block_y in blocks if block_z and block_y == 0]:
+        for dz in sorted([block_z for block_z, block_y in blocks if block_z and block_y == 0], key=lambda block_z: -abs(block_z)):
             c = remote(zsend.at[(z + dz + nz) % nz], zrecv.at[dz % nz], z_send.at[dz % nz], z_recv.at[dz % nz], at_tensor(dz, 0))
             c.start()
             zcs.append(c)
@@ -225,7 +227,7 @@
         core_forwards[half].append(c)
 
     def spread(half):
-        for k, (dyl, dx) in enumerate(others):
+        for k, (dyl, dx) in reversed(list(enumerate(others))):
             source = ((yl - dyl + nyl) % nyl) * nx + (x - dx + nx) % nx
             b = d_block(half, core, source)
             remote(b, b, d_send.at[half, k], d_recv.at[half, k], at_chip(dyl, dx)).wait_recv()
@@ -250,13 +252,9 @@
     hid = w.shape[0]
     cuts = list(range(0, hid, 256)) + [hid]
 
-    def weigh(half):
-        if half == 0:
-            for lo, hi in zip(cuts[:-1], cuts[1:]):
-                acc[lo:hi, :] = weight(0, lo, hi)
-            return
+    def weigh():
         for lo, hi in zip(cuts[:-1], cuts[1:]):
-            wg_ref[lo:hi, :] = (acc[lo:hi, :] + weight(1, lo, hi)).astype(BF16)
+            acc[lo:hi, :] = weight(0, lo, hi)
 
     start_gather()
     local_b()
@@ -271,26 +269,42 @@
     project(0)
     turn_ga()
     sum_b()
+    send_b(lay.order[:nz])
     reduce_send(0)
-    send_b(lay.order[:nz])
     for b in lay.order[nz:]:
         arrive(*b)
     send_b(lay.order[nz:])
     project(1)
     reduce_send(1)
+    g_out[...] = g[half_rows:2 * half_rows, :]
     activate(0)
     activate(1)
     spread(0)
     collect(0)
-    weigh(0)
+    weigh()
     spread(1)
     collect(1)
     finish_b()
-    weigh(1)
+    d_out[...] = d[half_rows:2 * half_rows, :]
     for c in sent + zcs + core_copies + chip_copies[0] + chip_copies[1] + delta_copies[0] + delta_copies[1]:
         c.wait_send()
     for c in core_forwards[0] + core_forwards[1]:
         c.wait_send()
+
+
+def finish_kernel(acc, d, g, ig, wg_hbm, ig_hbm, out, sem):
+    copies = [pltpu.make_async_copy(ig, ig_hbm, sem.at[0])]
+    copies[0].start()
+    hid = out.shape[0]
+    cuts = list(range(0, hid, 256)) + [hid]
+    for i, (lo, hi) in enumerate(zip(cuts[:-1], cuts[1:])):
+        product = lax.dot_general(d[:, lo:hi], g[...], (((0,), (0,)), ((), ())), preferred_element_type=F32)
+        out[lo:hi, :] = (acc[lo:hi, :] + product).astype(BF16)
+        c = pltpu.make_async_copy(out.at[pl.ds(lo, hi - lo)], wg_hbm.at[pl.ds(lo, hi - lo)], sem.at[1 + i])
+        c.start()
+        copies.append(c)
+    for c in copies:
+        c.wait()
 
 
 def build(mesh, lay):
@@ -305,11 +319,12 @@
         wide = -(-width // 256) * 128
         dma = pltpu.SemaphoreType.DMA
         flops = 2 * hid * width * (4 * half_rows + seq_b)
-        return pl.pallas_call(
+        parts = pl.pallas_call(
             functools.partial(kernel, lay, rows),
-            out_shape=(jax.ShapeDtypeStruct((hid, width), BF16), jax.ShapeDtypeStruct((depth, width), BF16)),
+            out_shape=(jax.ShapeDtypeStruct((hid, width), F32), jax.ShapeDtypeStruct((half_rows, hid), BF16),
+                       jax.ShapeDtypeStruct((half_rows, width), BF16), jax.ShapeDtypeStruct((depth, width), BF16)),
             in_specs=[pl.BlockSpec(memory_space=pl.ANY)] * 4,
-            out_specs=(pl.BlockSpec(memory_space=pltpu.VMEM), pl.BlockSpec(memory_space=pltpu.VMEM)),
+            out_specs=(pl.BlockSpec(memory_space=pltpu.VMEM),) * 4,
             scratch_shapes=[
                 pltpu.VMEM((hid, width), BF16),
                 pltpu.VMEM((2 * half_rows, width), BF16),
@@ -329,7 +344,6 @@
                 pltpu.VMEM((2, half_rows // 2, hid), BF16),
                 pltpu.VMEM((2, n, rows, hid), BF16),
                 pltpu.VMEM((2 * half_rows, hid), BF16),
-                pltpu.VMEM((hid, width), F32),
                 dma((5,)), dma((2 * nz,)), dma((2 * nz,)), dma, dma, dma((nz,)), dma((nz,)),
                 dma((2,)), dma((2,)), dma((2, n)), dma((2, n)), dma((2, n)), dma((2, n)), dma((2, n + 1)), dma((2, n + 1)),
             ],
@@ -337,6 +351,14 @@
                 collective_id=0, has_side_effects=True, vmem_limit_bytes=36 * 1024 * 1024),
             cost_estimate=pl.CostEstimate(flops=flops, bytes_accessed=5_000_000, transcendentals=100_000),
         )(*[pltpu.with_memory_space_constraint(v, pltpu.HBM) for v in (w_up, inputs_a, grad_a.T, grad_b.T)])
+        return pl.pallas_call(
+            finish_kernel,
+            out_shape=(jax.ShapeDtypeStruct((hid, width), BF16), jax.ShapeDtypeStruct((depth, width), BF16)),
+            in_specs=[pl.BlockSpec(memory_space=pltpu.VMEM)] * 4,
+            out_specs=(pl.BlockSpec(memory_space=pltpu.HBM),) * 2,
+            scratch_shapes=[pltpu.VMEM((hid, width), BF16), dma((8,))],
+            compiler_params=pltpu.CompilerParams(vmem_limit_bytes=16 * 1024 * 1024),
+        )(*parts)
 
     return jax.shard_map(
         step,

time: 55.3 us -> 54.8 us (level)
  local copies, waits for them, and re-layouts: 1.86 us -> 0 us
  Pallas kernels: 52.6 us -> 54 us
    unnamed x2 -> x0, local copies, waits for them, and re-layouts: 1.86 us -> none
    pallas_call x0 -> x1, Pallas kernels: none -> 1.65 us  [step(): pl.pallas_call(finish_kernel, out_shape=(jax.ShapeDtypeStruct((hid, width...]
where the time goes in v5:
time: 54.8 us; the launch traced here: 54.6 us
  Pallas kernels  54 us (99%)
  between operations  0.64 us (1%)
    pallas_call x1, Pallas kernels, step(): pl.pallas_call(functools.partial(kernel, lay, rows), out_shape=(jax.Shape...  52.4 us
    pallas_call x1, Pallas kernels, step(): pl.pallas_call(finish_kernel, out_shape=(jax.ShapeDtypeStruct((hid, width...  1.65 us

profile of v5, /device:TPU:1, one launch (start us, length us, event | category | flops | bytes accessed | tf_op | source)
XLA Modules:
  0.0 54.6 jit_solution(11895628776939484726)
XLA Ops:
  0.6 52.4 %shard_map.59 = (f32[928,928]{1,0:T(8,128)S(1)}, bf16[256,928]{1,0:T(8,128)(2,1)S(1)}, bf16[256,928]{1,0:T(8,128)(2,1)S(1)}, bf16[8,928]{1,0:T(8,128)(2,1)S(1)}) custom-call(bf16[928,928]{1,0:T(8,128)(2,1)} %w_hbm.1, bf16[16,928]{1,0:T(8,128)(2,1)} %a_hbm.1, bf16[928,512]{1,0:T(8,128)(2,1)} %bitcast.2, bf16[928,256]{1,0:T(8,128)(2,1)} %bitcast.3), custom_call_target="tpu_custom_call" | custom-call | flops 2204631040 | bytes 5000000 | tf_op jit(solution)/shard_map/pallas_call | solution.py:322
  53.0 1.6 %shard_map.60 = (bf16[928,928]{1,0:T(8,128)(2,1)}, bf16[8,928]{1,0:T(8,128)(2,1)}) custom-call(f32[928,928]{1,0:T(8,128)S(1)} %get-tuple-element.6.acc, bf16[256,928]{1,0:T(8,128)(2,1)S(1)} %get-tuple-element.7.d, bf16[256,928]{1,0:T(8,128)(2,1)S(1)} %get-tuple-element.8.g, bf16[8,928]{1,0:T(8,128)(2,1)S(1)} %get-tuple-element.9.ig), custom_call_target="tpu_custom_call" | custom-call | tf_op jit(solution)/shard_map/pallas_call | solution.py:354
